TPU v7x, 32 devices: a whole 2x2x4 slice. The times are simulated.
32 devices in a mesh: groups: 2 (over x), wide: 16 (over z, y, core).
Axes of the slice: x: 2, y: 2, z: 4, core: 2. Of those that a mesh axis runs over, the one named last changes fastest.
Arguments:
- tokens: bfloat16 [768, 8192], P(('groups', 'wide')), parts along dimension 0, may hold values from -6 to 6
- gate_weight: bfloat16 [8192, 14336], P(None, 'wide'), may hold values from -0.0625 to 0.0625
- up_weight: bfloat16 [8192, 14336], P(None, 'wide'), may hold values from -0.0625 to 0.0625
- adapter_in: bfloat16 [32, 64, 8192], P(('groups', 'wide')), parts along dimension 0, may hold values from -0.0625 to 0.0625
- adapter_out: bfloat16 [32, 64, 14336], P('groups', None, 'wide'), parts along dimension 0, may hold values from -0.75 to 0.75
- seg_adapter: int32 [6], P('groups'), parts along dimension 0, may hold values from 0 to 15
- holder_slot: int32 [32], P('groups'), parts along dimension 0, may hold values from 0 to 15, each once
- seg_length: int32 [6], P('groups'), parts along dimension 0, may hold values from 1 to 128, 288 in all
Outputs:
- hidden: bfloat16 [768, 14336], P('groups', 'wide'), parts along dimension 0
There are 2 independent parts, one for each index of `groups`. A program takes and returns all parts, laid end to end along the dimension named above; an argument that names none is the same for every part. Nothing has to cross between parts.
Inputs may be any that keep to these rules, and one draw needn't show every extreme that they name: `seg_adapter`: an adapter id below 16; several segments may name the same adapter. `holder_slot`: each slot once; the input map of slot k lives on device k // 1 of wide, as that device's local adapter k % 1. `seg_length`: the live rows stand first in their segment.
All inputs are finite; a program needn't handle non-finite values.
Results may differ from a plain program's by a relative error of at most 0.0035.
Values may be sent and summed in bfloat16 or wider, within the bound.
A program may use at most 128 MiB of HBM per device.

v0:
```python
import jax
import jax.numpy as jnp
from jax import lax
from jax.sharding import PartitionSpec as P

adapter_scale = 0.5


def on_device(
    tokens, gate_weight, up_weight, adapter_in, adapter_out, seg_adapter, holder_slot, seg_length
):
    holders = lax.axis_size("wide")
    my_index = lax.axis_index("wide")
    held_count = adapter_in.shape[0]
    rank_size = adapter_in.shape[1]
    model_dim = tokens.shape[1]
    row_count = tokens.shape[0] * holders
    seg_count = seg_adapter.shape[0]
    seg_size = row_count // seg_count
    columns = gate_weight.shape[1]
    pool_size = holder_slot.shape[0]
    matches = seg_adapter[:, None] == jnp.arange(pool_size, dtype=jnp.int32)[None, :]
    seg_slot = jnp.sum(jnp.where(matches, holder_slot[None, :], 0), axis=1)
    seg_owner = seg_slot // held_count
    local_slot = seg_slot % held_count
    gathered = lax.all_gather(tokens, "wide", axis=0, tiled=True)
    gate_block = jnp.dot(gathered, gate_weight, preferred_element_type=jnp.float32)
    up_weight_block = jnp.dot(gathered, up_weight, preferred_element_type=jnp.float32)

    def per_segment(operand):
        seg_rows, owner_now, slot_now = operand

        def compute():
            return lax.dot_general(
                seg_rows,
                adapter_in[slot_now],
                (((1,), (1,)), ((), ())),
                preferred_element_type=jnp.float32,
            )

        def nothing():
            return jnp.zeros((seg_size, rank_size), jnp.float32)

        return lax.cond(owner_now == my_index, compute, nothing)

    seg_blocks = gathered.reshape(seg_count, seg_size, model_dim)
    partial_in = lax.map(per_segment, (seg_blocks, seg_owner, local_slot)).reshape(
        row_count, rank_size
    )
    reduced_rank_state = lax.psum(partial_in, "wide").astype(jnp.bfloat16)
    selected_output = adapter_out[seg_slot]
    adapter_term = jnp.einsum(
        "iyg,ign->iyn",
        reduced_rank_state.reshape(seg_count, seg_size, rank_size),
        selected_output,
        preferred_element_type=jnp.float32,
    ).reshape(row_count, columns)
    up_output_total = up_weight_block + adapter_scale * adapter_term
    positions = jnp.arange(seg_size, dtype=jnp.int32)
    live_rows = (positions[None, :] < seg_length[:, None]).reshape(row_count)
    hidden = jnp.where(
        live_rows[:, None], jax.nn.silu(gate_block) * up_output_total, jnp.float32(0.0)
    )
    return hidden.astype(jnp.bfloat16)


def solution(mesh):
    in_specs = (
        P(("groups", "wide"), None),
        P(None, "wide"),
        P(None, "wide"),
        P(("groups", "wide"), None, None),
        P("groups", None, "wide"),
        P("groups"),
        P("groups"),
        P("groups"),
    )
    out_specs = P("groups", "wide")
    return jax.shard_map(
        on_device, mesh=mesh, in_specs=in_specs, out_specs=out_specs, check_vma=False
    )
```

profile of v0, /device:TPU:0, one launch (start us, length us, event | category | flops | bytes accessed | tf_op | source)
XLA Modules:
  0.0 170.1 jit_solution(2819872931671387241)
XLA Ops:
  6.5 0.0 copy-start
  6.5 0.0 all-gather.2.cloned.1.call-start
  6.5 0.7 all-gather.2.cloned.1.call-update
  7.3 0.9 select_reduce_fusion
  8.1 0.0 copy-done
  8.2 0.6 gather_fusion
  8.8 0.7 fusion.13
  9.5 64.7 %all-gather.2.cloned.1.call-done = bf16[384,8192]{1,0:T(8,128)(2,1)} async-done(((bf16[24,8192]{1,0:T(8,128)(2,1)}), bf16[384,8192]{1,0:T(8,128)(2,1)}) %all-gather.2.cloned.1.call-update) | async-done | bytes 6291472 | tf_op jit(solution)/shard_map/all_gather | solution.py:26
  74.2 4.4 %while.11 = (s32[]{:T(128)}, f32[3,128,64]{1,0,2:T(4,128)S(1)}, s32[3]{0:T(128)S(1)}, s32[]{:T(128)}, bf16[3,128,8192]{2,1,0:T(8,128)(2,1)}, /*index=5*/bf16[1,64,8192]{2,1,0:T(8,128)(2,1)}, s32[]{:T(128)}, s32[]{:T(128)}) while((s32[]{:T(128)}, f32[3,128,64]{1,0,2:T(4,128)S(1)}, s32[3]{0:T(128)S(1)}, s32[]{:T(128)}, ...), condition=%wide.region_4.5_spmd, body=%wide.region_1.4_spmd.sunk | while | flops 134217728 | bytes 3244699 | solution.py:47
  74.2 0.6 dynamic_slice.21
  75.5 0.2 dynamic_update_slice.6
  75.7 0.6 dynamic_slice.21
  77.0 0.2 dynamic_update_slice.6
  77.2 0.6 dynamic_slice.21
  78.4 0.2 dynamic_update_slice.6
  78.6 60.2 %psum.7 = bf16[384,64]{0,1:T(8,128)(2,1)S(1)} all-reduce(f32[384,64]{0,1:T(8,128)S(1)} %bitcast.51), channel_id=1, replica_groups=mesh['groups'=2,'wide'=16] {'wide'}, use_global_device_ids=true, to_apply=%region_5.6 | all-reduce | flops 24576 | bytes 147456 | tf_op jit(solution)/shard_map/psum | solution.py:50
  138.8 0.0 slice-start
  138.8 0.0 slice-start.2
  138.9 0.4 convolution_multiply_fusion
  139.3 0.0 slice-start.1
  139.3 0.0 slice-start.3
  139.3 0.0 slice-start.4
  139.3 0.0 slice-start.5
  139.3 16.3 %fusion.15 = f32[384,896]{1,0:T(8,128)S(1)} fusion(bf16[384,8192]{1,0:T(8,128)(2,1)} %bitcast.45, bf16[8192,896]{1,0:T(8,128)(2,1)} %param.13), kind=kOutput, calls=%fused_computation.23 | convolution fusion | flops 5637144576 | bytes 22347776 | tf_op jit(solution)/shard_map/dot_general | solution.py:27
  155.6 0.0 slice-done
  155.6 0.0 slice-done.2
  155.6 0.0 slice-done.1
  155.6 0.0 slice-done.3
  155.6 0.0 slice-done.4
  155.6 0.0 slice-done.5
  155.6 7.6 %fusion.10 = bf16[384,896]{1,0:T(8,128)(2,1)} fusion(f32[384,896]{1,0:T(8,128)S(1)} %bitcast.50, bf16[384,8192]{1,0:T(8,128)(2,1)S(1)} %bitcast.48, bf16[8192,896]{1,0:T(8,128)(2,1)S(1)} %bitcast.54, f32[384,896]{1,0:T(8,128)S(1)} %fusion.15, pred[384]{0:T(512)(128)(4,1)S(1)} %fusion.13), kind=kOutput, calls=%fused_computation.11 | convolution fusion | flops 5639897088 | bytes 24412544 | tf_op jit(solution)/shard_map/dot_general | solution.py:28
  (12 shorter events, 0.1 us)
Async XLA Ops:
  6.5 1.6 copy-start
  6.5 67.7 %all-gather.2.cloned.1.call-start = ((), (), s32[]{:S(2)}) async-start(), calls=%async_computation | async-start | bytes 6684672 | tf_op jit(solution)/shard_map/all_gather | solution.py:26
  138.8 16.7 %slice-start = ((s8[6291456]{0:T(1024)(128)(4,1)}), s8[4194304]{0:T(1024)(128)(4,1)S(1)}, s32[]{:S(2)}) async-start(s8[6291456]{0:T(1024)(128)(4,1)} %bitcast.46), calls=%async_computation.1 | async-start | bytes 8388608
  138.8 16.7 %slice-start.2 = ((s8[14680064]{0:T(1024)(128)(4,1)}), s8[4194304]{0:T(1024)(128)(4,1)S(1)}, s32[]{:S(2)}) async-start(s8[14680064]{0:T(1024)(128)(4,1)} %bitcast.53), calls=%async_computation.3 | async-start | bytes 8388608
  139.3 16.3 %slice-start.1 = ((s8[6291456]{0:T(1024)(128)(4,1)}), s8[2097152]{0:T(1024)(128)(4,1)S(1)}, s32[]{:S(2)}) async-start(s8[6291456]{0:T(1024)(128)(4,1)} %bitcast.46), calls=%async_computation.2 | async-start | bytes 4194304
  139.3 16.3 %slice-start.3 = ((s8[14680064]{0:T(1024)(128)(4,1)}), s8[4194304]{0:T(1024)(128)(4,1)S(1)}, s32[]{:S(2)}) async-start(s8[14680064]{0:T(1024)(128)(4,1)} %bitcast.53), calls=%async_computation.4 | async-start | bytes 8388608
  139.3 16.3 %slice-start.4 = ((s8[14680064]{0:T(1024)(128)(4,1)}), s8[4194304]{0:T(1024)(128)(4,1)S(1)}, s32[]{:S(2)}) async-start(s8[14680064]{0:T(1024)(128)(4,1)} %bitcast.53), calls=%async_computation.5 | async-start | bytes 8388608
  139.3 16.3 %slice-start.5 = ((s8[14680064]{0:T(1024)(128)(4,1)}), s8[2097152]{0:T(1024)(128)(4,1)S(1)}, s32[]{:S(2)}) async-start(s8[14680064]{0:T(1024)(128)(4,1)} %bitcast.53), calls=%async_computation.6 | async-start | bytes 4194304
Sparse Core Ops, SparseCore 0:
  9.6 64.5 all-gather.1
where the time goes:
time: 174 us; the launch traced here: 170 us
  waiting for transfers between devices  65.4 us (38%)
  blocking collectives  60.2 us (35%)
  matrix products  24.3 us (14%)
  between operations  13.6 us (8%)
  local copies, waits for them, and re-layouts  3 us (2%)
  loops' own time  2.05 us (1%)
    all_gather x1, waiting for transfers between devices, on_device(): gathered = lax.all_gather(tokens, 'wide', axis=0, tiled=True)  64.7 us
    psum x1, blocking collectives, on_device(): reduced_rank_state = lax.psum(partial_in, 'wide').astype(jnp.bfloat16)  60.2 us
    dot_general x1, matrix products, on_device(): jnp.dot(gathered, gate_weight, preferred_element_type=jnp.float32)  16.3 us
    dot_general x1, matrix products, on_device(): jnp.dot(gathered, up_weight, preferred_element_type=jnp.float32)  7.61 us
  transfers between devices with their start and end apart: 1, of which 1 were waited for; matrix products, arithmetic and copies ran while one was open for 1% of the time, Pallas kernels for 0%

commit v1 on v0

--- a/solution.py
+++ b/solution.py
@@ -1,12 +1,341 @@
+import functools
+
 import jax
 import jax.numpy as jnp
 from jax import lax
+from jax.experimental import pallas as pl
+from jax.experimental.pallas import tpu as pltpu
 from jax.sharding import PartitionSpec as P
 
 adapter_scale = 0.5
-
-
-def on_device(
+MESH = pl.DeviceIdType.MESH
+WINDOWS = 4
+PARTS = 2
+
+
+def kernel(
+    n, seg_count,
+    seg_adapter, holder_slot, seg_length, tokens, gate_weight, up_weight, adapter_in, adapter_out,
+    hidden,
+    gathered, weights, inmap, outmap, acc, low_acc, swap_out, swap_in, low_parts, low_sum,
+    weight_sem, map_sem, swap_sem, ring_send, ring_recv, pair_send, pair_recv,
+    low_send, low_recv, all_send, all_recv,
+):
+    me = lax.axis_index("wide")
+    chips = n // 2
+    depth = chips // 2
+    steps = chips - 1
+    chip, core = me // 2, me % 2
+    zi, yi = chip // 2, chip % 2
+    pos = zi + yi * (2 * depth - 1 - 2 * zi)
+    pair = chip * 2 + 1 - core
+    rows, columns = hidden.shape
+    chip_rows = rows // chips
+    own_rows = rows // n
+    half_dim = tokens.shape[1] // 2
+    width = gathered.shape[-1]
+    part = width // PARTS
+    seg_size = rows // seg_count
+
+    def chip_at(q):
+        side = q // depth
+        return (q + side * (2 * depth - 1 - 2 * q)) * 2 + side
+
+    def block_of(half, way, win):
+        return (half * 2 + way) * WINDOWS + win
+
+    def weight_copy(mat, half, way, win):
+        block = block_of(half, way, win)
+        source = (gate_weight, up_weight)[mat]
+        return pltpu.make_async_copy(
+            source.at[pl.ds(pl.multiple_of(block * width, width), width), :],
+            weights.at[mat, block],
+            weight_sem.at[mat, block],
+        )
+
+    inmap_copy = pltpu.make_async_copy(adapter_in.at[0], inmap, map_sem.at[0])
+    outmap_copy = pltpu.make_async_copy(adapter_out, outmap, map_sem.at[1])
+
+    barrier = pltpu.get_barrier_semaphore()
+    for i in range(1, n):
+        pl.semaphore_signal(
+            barrier, inc=1, device_id={"wide": lax.rem(me + i, n)}, device_id_type=MESH
+        )
+    other = tokens[:, pl.ds(pl.multiple_of((1 - core) * half_dim, half_dim), half_dim)]
+    pad = jnp.zeros((swap_out.shape[0] - own_rows, half_dim), jnp.float32)
+    swap_out[...] = jnp.concatenate([other.astype(jnp.float32), pad], axis=0).astype(jnp.bfloat16)
+    pl.semaphore_wait(barrier, n - 1)
+
+    swap = pltpu.make_async_remote_copy(
+        src_ref=swap_out, dst_ref=swap_in, send_sem=swap_sem.at[0], recv_sem=swap_sem.at[1],
+        device_id={"wide": pair}, device_id_type=MESH,
+    )
+    swap.start()
+    inmap_copy.start()
+    for win in range(WINDOWS):
+        for half in range(2):
+            for way in range(2):
+                for mat in range(2):
+                    weight_copy(mat, half, way, win).start()
+    outmap_copy.start()
+    swap.wait()
+
+    def rows_of(origin):
+        return pl.ds(pl.multiple_of(chip_at(origin) * chip_rows, 16), chip_rows)
+
+    def ring_copy(way, win, cut, step, origin):
+        sign = 1 - 2 * way
+        target = chip_at((pos + sign + chips) % chips) * 2 + core
+        place = gathered.at[core, way, win, rows_of(origin), pl.ds(cut * part, part)]
+        return pltpu.make_async_remote_copy(
+            src_ref=place, dst_ref=place,
+            send_sem=ring_send.at[way, win, cut, step], recv_sem=ring_recv.at[way, win, cut, step],
+            device_id={"wide": target}, device_id_type=MESH,
+        )
+
+    def pair_copy(half, way, win, step, origin):
+        place = gathered.at[half, way, win, rows_of(origin), :]
+        return pltpu.make_async_remote_copy(
+            src_ref=place, dst_ref=place,
+            send_sem=pair_send.at[way, win, step], recv_sem=pair_recv.at[way, win, step],
+            device_id={"wide": pair}, device_id_type=MESH,
+        )
+
+    def origin_at(way, step):
+        sign = 1 - 2 * way
+        return (pos - sign * step + 2 * chips) % chips
+
+    def send_own(win):
+        for cut in range(PARTS):
+            for way in range(2):
+                ring_copy(way, win, cut, 0, pos).start()
+        for way in range(2):
+            pair_copy(core, way, win, 0, pos).start()
+
+    for win in range(WINDOWS):
+        for way in range(2):
+            at = (way * WINDOWS + win) * width
+            mine = tokens[:, pl.ds(pl.multiple_of(core * half_dim + at, width), width)]
+            mine = mine.astype(jnp.float32)
+            theirs = swap_in[:, at:at + width].astype(jnp.float32)[:own_rows]
+            first = jnp.where(core == 0, mine, theirs)
+            second = jnp.where(core == 0, theirs, mine)
+            gathered[core, way, win, rows_of(pos), :] = jnp.concatenate(
+                [first, second], axis=0
+            ).astype(jnp.bfloat16)
+        if win == 0:
+            send_own(0)
+
+    acc[...] = jnp.zeros_like(acc)
+    low_acc[...] = jnp.zeros_like(low_acc)
+    inmap_copy.wait()
+
+    def wait_pair(way, win):
+        def one(step, carry):
+            pair_copy(1 - core, way, win, step, origin_at(way, step)).wait_recv()
+            return carry
+        lax.fori_loop(0, chips, one, 0)
+
+    def low_piece(win, half, way):
+        at = pl.multiple_of(block_of(half, way, win) * width, width)
+        low_acc[...] += lax.dot_general(
+            gathered[half, way, win], inmap[:, pl.ds(at, width)],
+            (((1,), (1,)), ((), ())), preferred_element_type=jnp.float32,
+        )
+
+    def main_piece(win, index, with_low):
+        mat, way, half = index % 2, (index // 2) % 2, (core + index // 4) % 2
+        block = block_of(half, way, win)
+        if with_low:
+            @pl.when((mat == 0) & (index >= 4))
+            def _():
+                wait_pair(way, win)
+
+            @pl.when(mat == 0)
+            def _():
+                low_piece(win, half, way)
+        pltpu.make_async_copy(
+            gate_weight.at[pl.ds(0, width), :], weights.at[mat, block], weight_sem.at[mat, block]
+        ).wait()
+        acc[mat] += jnp.dot(
+            gathered[half, way, win], weights[mat, block], preferred_element_type=jnp.float32
+        )
+
+    def round_of(t, carry):
+        win, step = t // steps, t % steps
+        for cut in range(PARTS):
+            for way in range(2):
+                origin = origin_at(way, step + 1)
+                ring_copy(way, win, cut, step, origin).wait_recv()
+
+                @pl.when(step < steps - 1)
+                def _():
+                    ring_copy(way, win, cut, step + 1, origin).start()
+        for way in range(2):
+            pair_copy(core, way, win, step + 1, origin_at(way, step + 1)).start()
+
+        @pl.when((step == steps - 2) & (win < WINDOWS - 1))
+        def _():
+            send_own(win + 1)
+
+        @pl.when(win > 0)
+        def _():
+            first = (step * 8) // steps
+            count = ((step + 1) * 8) // steps - first
+
+            def piece(i, c):
+                main_piece(win - 1, first + i, True)
+                return c
+            lax.fori_loop(0, count, piece, 0)
+        return carry
+
+    lax.fori_loop(0, WINDOWS * steps, round_of, 0)
+
+    last = WINDOWS - 1
+    for way in range(2):
+        low_piece(last, core, way)
+    for way in range(2):
+        wait_pair(way, last)
+        low_piece(last, 1 - core, way)
+
+    slots = [holder_slot[seg_adapter[s]] for s in range(seg_count)]
+    kept = jnp.concatenate(
+        [
+            jnp.where(slots[s] == me, low_acc[s * seg_size:(s + 1) * seg_size, :], 0.0)
+            for s in range(seg_count)
+        ],
+        axis=0,
+    )
+    low_acc[...] = kept
+
+    def own_slice(device):
+        return pl.ds(pl.multiple_of(device * own_rows, 8), own_rows)
+
+    def low_copy(i):
+        target = lax.rem(me + i, n)
+        return pltpu.make_async_remote_copy(
+            src_ref=low_acc.at[own_slice(target), :], dst_ref=low_parts.at[i],
+            send_sem=low_send.at[i], recv_sem=low_recv.at[i],
+            device_id={"wide": target}, device_id_type=MESH,
+        )
+
+    def all_copy(i):
+        target = lax.rem(me + i, n)
+        place = low_sum.at[own_slice(me), :]
+        return pltpu.make_async_remote_copy(
+            src_ref=place, dst_ref=place, send_sem=all_send.at[i], recv_sem=all_recv.at[i],
+            device_id={"wide": target}, device_id_type=MESH,
+        )
+
+    def all_arrived(i):
+        place = low_sum.at[own_slice(lax.rem(me + n - i, n)), :]
+        return pltpu.make_async_remote_copy(
+            src_ref=place, dst_ref=place, send_sem=all_send.at[i], recv_sem=all_recv.at[i],
+            device_id={"wide": lax.rem(me + i, n)}, device_id_type=MESH,
+        )
+
+    for i in range(1, n):
+        low_copy(i).start()
+
+    def early(i, c):
+        main_piece(last, i, False)
+        return c
+
+    lax.fori_loop(0, 4, early, 0)
+    for i in range(1, n):
+        low_copy(i).wait_recv()
+    total = low_acc[own_slice(me), :]
+    for i in range(1, n):
+        total = total + low_parts[i]
+    low_sum[own_slice(me), :] = total
+    for i in range(1, n):
+        all_copy(i).start()
+    lax.fori_loop(4, 8, early, 0)
+    acc[0] = acc[0] / (1.0 + jnp.exp(-acc[0]))
+    outmap_copy.wait()
+    for i in range(1, n):
+        all_arrived(i).wait_recv()
+    for s in range(seg_count):
+        at = s * seg_size
+        low = low_sum[at:at + seg_size, :].astype(jnp.bfloat16)
+        term = jnp.dot(low, outmap[slots[s]], preferred_element_type=jnp.float32)
+        value = acc[0, at:at + seg_size, :] * (
+            acc[1, at:at + seg_size, :] + adapter_scale * term
+        )
+        position = lax.broadcasted_iota(jnp.int32, value.shape, 0)
+        hidden[at:at + seg_size, :] = jnp.where(
+            position < seg_length[s], value, 0.0
+        ).astype(hidden.dtype)
+
+    for i in range(1, n):
+        low_copy(i).wait_send()
+        all_copy(i).wait_send()
+
+    def drain(t, carry):
+        win, step = t // steps, t % steps
+        for way in range(2):
+            for cut in range(PARTS):
+                ring_copy(way, win, cut, step, pos).wait_send()
+            pair_copy(core, way, win, step, pos).wait_send()
+
+            @pl.when(step == 0)
+            def _():
+                pair_copy(core, way, win, steps, pos).wait_send()
+        return carry
+
+    lax.fori_loop(0, WINDOWS * steps, drain, 0)
+
+
+def fused(
+    tokens, gate_weight, up_weight, adapter_in, adapter_out, seg_adapter, holder_slot, seg_length
+):
+    n = lax.axis_size("wide")
+    rows = tokens.shape[0] * n
+    dim = tokens.shape[1]
+    columns = gate_weight.shape[1]
+    rank = adapter_in.shape[1]
+    chips = n // 2
+    width = dim // 4 // WINDOWS
+    dma = pltpu.SemaphoreType.DMA
+    smem = pl.BlockSpec(memory_space=pltpu.SMEM)
+    hbm = pl.BlockSpec(memory_space=pl.ANY)
+    vmem = pl.BlockSpec(memory_space=pltpu.VMEM)
+    return pl.pallas_call(
+        functools.partial(kernel, n, seg_adapter.shape[0]),
+        out_shape=jax.ShapeDtypeStruct((rows, columns), jnp.bfloat16),
+        in_specs=[smem, smem, smem, vmem, hbm, hbm, hbm, hbm],
+        out_specs=vmem,
+        scratch_shapes=[
+            pltpu.VMEM((2, 2, WINDOWS, rows, width), jnp.bfloat16),
+            pltpu.VMEM((2, 4 * WINDOWS, width, columns), jnp.bfloat16),
+            pltpu.VMEM((rank, dim), jnp.bfloat16),
+            pltpu.VMEM(adapter_out.shape, jnp.bfloat16),
+            pltpu.VMEM((2, rows, columns), jnp.float32),
+            pltpu.VMEM((rows, rank), jnp.float32),
+            pltpu.VMEM((32, dim // 2), jnp.bfloat16),
+            pltpu.VMEM((32, dim // 2), jnp.bfloat16),
+            pltpu.VMEM((n, rows // n, rank), jnp.float32),
+            pltpu.VMEM((rows, rank), jnp.float32),
+            dma((2, 4 * WINDOWS)),
+            dma((2,)),
+            dma((2,)),
+            dma((2, WINDOWS, PARTS, chips - 1)),
+            dma((2, WINDOWS, PARTS, chips - 1)),
+            dma((2, WINDOWS, chips)),
+            dma((2, WINDOWS, chips)),
+            dma((n,)),
+            dma((n,)),
+            dma((n,)),
+            dma((n,)),
+        ],
+        compiler_params=pltpu.CompilerParams(
+            collective_id=0, has_side_effects=True, vmem_limit_bytes=60 * 1024 * 1024
+        ),
+        name="gated_input",
+    )(seg_adapter, holder_slot, seg_length, tokens, gate_weight, up_weight, adapter_in, adapter_out)
+
+
+def plain(
     tokens, gate_weight, up_weight, adapter_in, adapter_out, seg_adapter, holder_slot, seg_length
 ):
     holders = lax.axis_size("wide")
@@ -64,6 +393,22 @@
     return hidden.astype(jnp.bfloat16)
 
 
+def on_device(tokens, gate_weight, up_weight, adapter_in, *rest):
+    n = lax.axis_size("wide")
+    own_rows, dim = tokens.shape
+    resident = 2 * (2 * dim * gate_weight.shape[1] + own_rows * n * dim)
+    fits = (
+        n % 4 == 0
+        and gate_weight.shape[1] % 128 == 0
+        and own_rows % 8 == 0
+        and own_rows <= 32
+        and adapter_in.shape[0] == 1
+        and dim % (4 * WINDOWS * PARTS * 128) == 0
+        and resident < 40 * 1024 * 1024
+    )
+    return (fused if fits else plain)(tokens, gate_weight, up_weight, adapter_in, *rest)
+
+
 def solution(mesh):
     in_specs = (
         P(("groups", "wide"), None),

time: 174 us -> 113 us (0.65); the launches traced: 170 us -> 112 us
  Pallas kernels: 0 us -> 110 us
  waiting for transfers between devices: 65.4 us -> 0 us
  blocking collectives: 60.2 us -> 0 us
  matrix products: 24.3 us -> 0 us
  between operations: 13.6 us -> 0.01 us
  loops' own time: 2.05 us -> 0 us
    pallas_call x0 -> x1, Pallas kernels: none -> 110 us  [fused(): pl.pallas_call(functools.partial(kernel, n, seg_adapter.shape[0]), out_sh...]
    all_gather x1 -> x0, waiting for transfers between devices: 64.7 us -> none  [on_device(): gathered = lax.all_gather(tokens, 'wide', axis=0, tiled=True)]
    psum x1 -> x0, blocking collectives: 60.2 us -> none  [on_device(): reduced_rank_state = lax.psum(partial_in, 'wide').astype(jnp.bfloat16)]
    dot_general x3 -> x0, matrix products: 24.3 us -> none  [the longest x1 16.3 us: on_device(): jnp.dot(gathered, gate_weight, preferred_element_type=jnp.float32)]
    another operation x4 -> x0, loops' own time: 2.05 us -> none  [the longest x1 2 us: on_device(): lax.map(per_segment, (seg_blocks, seg_owner, local_slot))]
    unnamed x15 -> x1, local copies, waits for them, and re-layouts: 0.05 us -> 2 us
    dynamic_slice x3 -> x0, local copies, waits for them, and re-layouts: 1.82 us -> none  [on_device(): lax.map(per_segment, (seg_blocks, seg_owner, local_slot))]
  transfers between devices with their start and end apart: 1 -> 0, of which waited for: 1 -> 0; matrix products, arithmetic and copies ran while one was open for 1% -> 0% of each run, Pallas kernels for 0% -> 0%
where the time goes in v1:
time: 113 us; the launch traced here: 112 us
  Pallas kernels  110 us (97%)
  local copies, waits for them, and re-layouts  2 us (2%)
    pallas_call x1, Pallas kernels, fused(): pl.pallas_call(functools.partial(kernel, n, seg_adapter.shape[0]), out_sh...  110 us

profile of v1, /device:TPU:0, one launch (start us, length us, event | category | flops | bytes accessed | tf_op | source)
XLA Modules:
  0.0 112.4 jit_solution(1778649694927563814)
XLA Ops:
  0.0 110.4 %gated_input.1 = bf16[384,896]{1,0:T(8,128)(2,1)} custom-call(s32[3]{0:T(128)} %seg_adapter.1, s32[16]{0:T(128)} %holder_slot.1, s32[3]{0:T(128)} %seg_length.1, bf16[24,8192]{1,0:T(8,128)(2,1)} %tokens.1, bf16[8192,896]{1,0:T(8,128)(2,1)} %gate_weight.1, bf16[8192,896]{1,0:T(8,128)(2,1)} %up_weight.1, bf16[1,64,8192]{2,1,0:T(8,128)(2,1)} %adapter_in.1, ...), custom_call_target="tpu_custom_call" | custom-call | tf_op jit(solution)/shard_map/gated_input/pallas_call | solution.py:303
  110.4 2.0 %copy.10 = bf16[384,896]{1,0:T(8,128)(2,1)} copy(bf16[384,896]{1,0:T(8,128)(2,1)} %gated_input.1) | data formatting | bytes 1376256

commit v2 on v1

--- a/solution.py
+++ b/solution.py
@@ -9,8 +9,8 @@
 
 adapter_scale = 0.5
 MESH = pl.DeviceIdType.MESH
-WINDOWS = 4
-PARTS = 2
+WINDOWS = 1
+PARTS = 4
 
 
 def kernel(
@@ -36,6 +36,8 @@
     width = gathered.shape[-1]
     part = width // PARTS
     seg_size = rows // seg_count
+    rank = adapter_in.shape[1]
+    lanes = inmap.shape[0]
 
     def chip_at(q):
         side = q // depth
@@ -53,18 +55,20 @@
             weight_sem.at[mat, block],
         )
 
-    inmap_copy = pltpu.make_async_copy(adapter_in.at[0], inmap, map_sem.at[0])
+    inmap_copy = pltpu.make_async_copy(
+        adapter_in.at[0], inmap.at[pl.ds(0, rank), :], map_sem.at[0]
+    )
     outmap_copy = pltpu.make_async_copy(adapter_out, outmap, map_sem.at[1])
 
     barrier = pltpu.get_barrier_semaphore()
-    for i in range(1, n):
-        pl.semaphore_signal(
-            barrier, inc=1, device_id={"wide": lax.rem(me + i, n)}, device_id_type=MESH
-        )
+    after = chip_at((pos + 1) % chips) * 2 + core
+    before = chip_at((pos + chips - 1) % chips) * 2 + core
+    for neighbour in (pair, after, before):
+        pl.semaphore_signal(barrier, inc=1, device_id={"wide": neighbour}, device_id_type=MESH)
     other = tokens[:, pl.ds(pl.multiple_of((1 - core) * half_dim, half_dim), half_dim)]
     pad = jnp.zeros((swap_out.shape[0] - own_rows, half_dim), jnp.float32)
     swap_out[...] = jnp.concatenate([other.astype(jnp.float32), pad], axis=0).astype(jnp.bfloat16)
-    pl.semaphore_wait(barrier, n - 1)
+    pl.semaphore_wait(barrier, 3)
 
     swap = pltpu.make_async_remote_copy(
         src_ref=swap_out, dst_ref=swap_in, send_sem=swap_sem.at[0], recv_sem=swap_sem.at[1],
@@ -128,6 +132,8 @@
 
     acc[...] = jnp.zeros_like(acc)
     low_acc[...] = jnp.zeros_like(low_acc)
+    if lanes > rank:
+        inmap[rank:, :] = jnp.zeros((lanes - rank, inmap.shape[1]), inmap.dtype)
     inmap_copy.wait()
 
     def wait_pair(way, win):
@@ -257,7 +263,7 @@
         all_arrived(i).wait_recv()
     for s in range(seg_count):
         at = s * seg_size
-        low = low_sum[at:at + seg_size, :].astype(jnp.bfloat16)
+        low = low_sum[at:at + seg_size, :rank].astype(jnp.bfloat16)
         term = jnp.dot(low, outmap[slots[s]], preferred_element_type=jnp.float32)
         value = acc[0, at:at + seg_size, :] * (
             acc[1, at:at + seg_size, :] + adapter_scale * term
@@ -293,7 +299,7 @@
     rows = tokens.shape[0] * n
     dim = tokens.shape[1]
     columns = gate_weight.shape[1]
-    rank = adapter_in.shape[1]
+    lanes = -(-adapter_in.shape[1] // 128) * 128
     chips = n // 2
     width = dim // 4 // WINDOWS
     dma = pltpu.SemaphoreType.DMA
@@ -308,14 +314,14 @@
         scratch_shapes=[
             pltpu.VMEM((2, 2, WINDOWS, rows, width), jnp.bfloat16),
             pltpu.VMEM((2, 4 * WINDOWS, width, columns), jnp.bfloat16),
-            pltpu.VMEM((rank, dim), jnp.bfloat16),
+            pltpu.VMEM((lanes, dim), jnp.bfloat16),
             pltpu.VMEM(adapter_out.shape, jnp.bfloat16),
             pltpu.VMEM((2, rows, columns), jnp.float32),
-            pltpu.VMEM((rows, rank), jnp.float32),
+            pltpu.VMEM((rows, lanes), jnp.float32),
             pltpu.VMEM((32, dim // 2), jnp.bfloat16),
             pltpu.VMEM((32, dim // 2), jnp.bfloat16),
-            pltpu.VMEM((n, rows // n, rank), jnp.float32),
-            pltpu.VMEM((rows, rank), jnp.float32),
+            pltpu.VMEM((n, rows // n, lanes), jnp.float32),
+            pltpu.VMEM((rows, lanes), jnp.float32),
             dma((2, 4 * WINDOWS)),
             dma((2,)),
             dma((2,)),

time: 113 us -> 64 us (0.57)
  Pallas kernels: 110 us -> 61.8 us
    pallas_call x1, Pallas kernels: 110 us -> 61.8 us  [fused(): pl.pallas_call(functools.partial(kernel, n, seg_adapter.shape[0]), out_sh...]
where the time goes in v2:
time: 64 us; the launch traced here: 63.8 us
  Pallas kernels  61.8 us (97%)
  local copies, waits for them, and re-layouts  2 us (3%)
    pallas_call x1, Pallas kernels, fused(): pl.pallas_call(functools.partial(kernel, n, seg_adapter.shape[0]), out_sh...  61.8 us
    unnamed x1, local copies, waits for them, and re-layouts  2 us

profile of v2, /device:TPU:0, one launch (start us, length us, event | category | flops | bytes accessed | tf_op | source)
XLA Modules:
  0.0 63.8 jit_solution(11528341722080375229)
XLA Ops:
  0.0 61.8 %gated_input.1 = bf16[384,896]{1,0:T(8,128)(2,1)} custom-call(s32[3]{0:T(128)} %seg_adapter.1, s32[16]{0:T(128)} %holder_slot.1, s32[3]{0:T(128)} %seg_length.1, bf16[24,8192]{1,0:T(8,128)(2,1)} %tokens.1, bf16[8192,896]{1,0:T(8,128)(2,1)} %gate_weight.1, bf16[8192,896]{1,0:T(8,128)(2,1)} %up_weight.1, bf16[1,64,8192]{2,1,0:T(8,128)(2,1)} %adapter_in.1, ...), custom_call_target="tpu_custom_call" | custom-call | tf_op jit(solution)/shard_map/gated_input/pallas_call | solution.py:309
  61.8 2.0 %copy.10 = bf16[384,896]{1,0:T(8,128)(2,1)} copy(bf16[384,896]{1,0:T(8,128)(2,1)} %gated_input.1) | data formatting | bytes 1376256

commit v3 on v2

--- a/solution.py
+++ b/solution.py
@@ -87,18 +87,20 @@
     def rows_of(origin):
         return pl.ds(pl.multiple_of(chip_at(origin) * chip_rows, 16), chip_rows)
 
-    def ring_copy(way, win, cut, step, origin):
-        sign = 1 - 2 * way
-        target = chip_at((pos + sign + chips) % chips) * 2 + core
-        place = gathered.at[core, way, win, rows_of(origin), pl.ds(cut * part, part)]
+    def slot_rows(slot):
+        return pl.ds(pl.multiple_of(slot * chip_rows, 16), chip_rows)
+
+    def ring_copy(way, win, cut, step):
+        columns_of = pl.ds(cut * part, part)
         return pltpu.make_async_remote_copy(
-            src_ref=place, dst_ref=place,
+            src_ref=gathered.at[core, way, win, slot_rows(step), columns_of],
+            dst_ref=gathered.at[core, way, win, slot_rows(step + 1), columns_of],
             send_sem=ring_send.at[way, win, cut, step], recv_sem=ring_recv.at[way, win, cut, step],
-            device_id={"wide": target}, device_id_type=MESH,
-        )
-
-    def pair_copy(half, way, win, step, origin):
-        place = gathered.at[half, way, win, rows_of(origin), :]
+            device_id={"wide": (after, before)[way]}, device_id_type=MESH,
+        )
+
+    def pair_copy(half, way, win, step):
+        place = gathered.at[half, way, win, slot_rows(step), :]
         return pltpu.make_async_remote_copy(
             src_ref=place, dst_ref=place,
             send_sem=pair_send.at[way, win, step], recv_sem=pair_recv.at[way, win, step],
@@ -112,9 +114,9 @@
     def send_own(win):
         for cut in range(PARTS):
             for way in range(2):
-                ring_copy(way, win, cut, 0, pos).start()
+                ring_copy(way, win, cut, 0).start()
         for way in range(2):
-            pair_copy(core, way, win, 0, pos).start()
+            pair_copy(core, way, win, 0).start()
 
     for win in range(WINDOWS):
         for way in range(2):
@@ -124,7 +126,7 @@
             theirs = swap_in[:, at:at + width].astype(jnp.float32)[:own_rows]
             first = jnp.where(core == 0, mine, theirs)
             second = jnp.where(core == 0, theirs, mine)
-            gathered[core, way, win, rows_of(pos), :] = jnp.concatenate(
+            gathered[core, way, win, :chip_rows, :] = jnp.concatenate(
                 [first, second], axis=0
             ).astype(jnp.bfloat16)
         if win == 0:
@@ -136,73 +138,87 @@
         inmap[rank:, :] = jnp.zeros((lanes - rank, inmap.shape[1]), inmap.dtype)
     inmap_copy.wait()
 
-    def wait_pair(way, win):
-        def one(step, carry):
-            pair_copy(1 - core, way, win, step, origin_at(way, step)).wait_recv()
-            return carry
-        lax.fori_loop(0, chips, one, 0)
-
-    def low_piece(win, half, way):
-        at = pl.multiple_of(block_of(half, way, win) * width, width)
-        low_acc[...] += lax.dot_general(
-            gathered[half, way, win], inmap[:, pl.ds(at, width)],
+    group = chips // 2
+
+    def group_slots(which):
+        return pl.ds(pl.multiple_of(which * group * chip_rows, 16), group * chip_rows)
+
+    def wait_pair(which, way):
+        for k in range(group):
+            pair_copy(1 - core, way, 0, which * group + k).wait_recv()
+
+    def add_rows(target, which, way, value):
+        for k in range(group):
+            target[rows_of(origin_at(way, which * group + k)), :] += (
+                value[k * chip_rows:(k + 1) * chip_rows]
+            )
+
+    def low_piece(which, half, way):
+        at = pl.multiple_of(block_of(half, way, 0) * width, width)
+        value = lax.dot_general(
+            gathered[half, way, 0, group_slots(which), :], inmap[:, pl.ds(at, width)],
             (((1,), (1,)), ((), ())), preferred_element_type=jnp.float32,
         )
-
-    def main_piece(win, index, with_low):
+        add_rows(low_acc, which, way, value)
+
+    def main_piece(which, index, first):
         mat, way, half = index % 2, (index // 2) % 2, (core + index // 4) % 2
-        block = block_of(half, way, win)
-        if with_low:
+        block = block_of(half, way, 0)
+        if first:
             @pl.when((mat == 0) & (index >= 4))
             def _():
-                wait_pair(way, win)
+                wait_pair(which, way)
 
             @pl.when(mat == 0)
             def _():
-                low_piece(win, half, way)
-        pltpu.make_async_copy(
-            gate_weight.at[pl.ds(0, width), :], weights.at[mat, block], weight_sem.at[mat, block]
-        ).wait()
-        acc[mat] += jnp.dot(
-            gathered[half, way, win], weights[mat, block], preferred_element_type=jnp.float32
-        )
-
-    def round_of(t, carry):
-        win, step = t // steps, t % steps
-        for cut in range(PARTS):
-            for way in range(2):
-                origin = origin_at(way, step + 1)
-                ring_copy(way, win, cut, step, origin).wait_recv()
-
-                @pl.when(step < steps - 1)
+                low_piece(which, half, way)
+            pltpu.make_async_copy(
+                gate_weight.at[pl.ds(0, width), :], weights.at[mat, block],
+                weight_sem.at[mat, block],
+            ).wait()
+        value = jnp.dot(
+            gathered[half, way, 0, group_slots(which), :], weights[mat, block],
+            preferred_element_type=jnp.float32,
+        )
+        add_rows(acc.at[mat], which, way, value)
+
+    per_round = -(-8 // (steps - group + 1))
+
+    def round_of(step, carry):
+        for turn in range(2):
+            for cut in range(turn * PARTS // 2, (turn + 1) * PARTS // 2):
+                for way in range(2):
+                    ring_copy(way, 0, cut, step).wait_recv()
+
+                    @pl.when(step < steps - 1)
+                    def _():
+                        ring_copy(way, 0, cut, step + 1).start()
+            if turn == 1:
+                for way in range(2):
+                    pair_copy(core, way, 0, step + 1).start()
+
+            @pl.when(step >= group - 1)
+            def _():
+                begin = (step - group + 1) * per_round + turn * (per_round // 2)
+                count = per_round - per_round // 2 if turn else per_round // 2
+
+                def piece(i, c):
+                    @pl.when(begin + i < 8)
+                    def _():
+                        main_piece(0, begin + i, True)
+                    return c
+                @pl.when((step < steps - 1) | (turn == 0))
                 def _():
-                    ring_copy(way, win, cut, step + 1, origin).start()
-        for way in range(2):
-            pair_copy(core, way, win, step + 1, origin_at(way, step + 1)).start()
-
-        @pl.when((step == steps - 2) & (win < WINDOWS - 1))
-        def _():
-            send_own(win + 1)
-
-        @pl.when(win > 0)
-        def _():
-            first = (step * 8) // steps
-            count = ((step + 1) * 8) // steps - first
-
-            def piece(i, c):
-                main_piece(win - 1, first + i, True)
-                return c
-            lax.fori_loop(0, count, piece, 0)
+                    lax.fori_loop(0, count, piece, 0)
         return carry
 
-    lax.fori_loop(0, WINDOWS * steps, round_of, 0)
-
-    last = WINDOWS - 1
+    lax.fori_loop(0, steps, round_of, 0)
+
     for way in range(2):
-        low_piece(last, core, way)
+        low_piece(1, core, way)
     for way in range(2):
-        wait_pair(way, last)
-        low_piece(last, 1 - core, way)
+        wait_pair(1, way)
+        low_piece(1, 1 - core, way)
 
     slots = [holder_slot[seg_adapter[s]] for s in range(seg_count)]
     kept = jnp.concatenate(
@@ -242,9 +258,10 @@
 
     for i in range(1, n):
         low_copy(i).start()
+    main_piece(0, 7, True)
 
     def early(i, c):
-        main_piece(last, i, False)
+        main_piece(1, i, False)
         return c
 
     lax.fori_loop(0, 4, early, 0)
@@ -281,12 +298,12 @@
         win, step = t // steps, t % steps
         for way in range(2):
             for cut in range(PARTS):
-                ring_copy(way, win, cut, step, pos).wait_send()
-            pair_copy(core, way, win, step, pos).wait_send()
+                ring_copy(way, win, cut, step).wait_send()
+            pair_copy(core, way, win, step).wait_send()
 
             @pl.when(step == 0)
             def _():
-                pair_copy(core, way, win, steps, pos).wait_send()
+                pair_copy(core, way, win, steps).wait_send()
         return carry
 
     lax.fori_loop(0, WINDOWS * steps, drain, 0)

time: 64 us -> 58.9 us (0.920)
  Pallas kernels: 61.8 us -> 56.7 us
    pallas_call x1, Pallas kernels: 61.8 us -> 56.7 us  [fused(): pl.pallas_call(functools.partial(kernel, n, seg_adapter.shape[0]), out_sh...]
where the time goes in v3:
time: 58.9 us; the launch traced here: 58.7 us
  Pallas kernels  56.7 us (96%)
  local copies, waits for them, and re-layouts  2 us (3%)
    pallas_call x1, Pallas kernels, fused(): pl.pallas_call(functools.partial(kernel, n, seg_adapter.shape[0]), out_sh...  56.7 us
    unnamed x1, local copies, waits for them, and re-layouts  2 us

profile of v3, /device:TPU:0, one launch (start us, length us, event | category | flops | bytes accessed | tf_op | source)
XLA Modules:
  0.0 58.7 jit_solution(10503087447802734281)
XLA Ops:
  0.0 56.7 %gated_input.1 = bf16[384,896]{1,0:T(8,128)(2,1)} custom-call(s32[3]{0:T(128)} %seg_adapter.1, s32[16]{0:T(128)} %holder_slot.1, s32[3]{0:T(128)} %seg_length.1, bf16[24,8192]{1,0:T(8,128)(2,1)} %tokens.1, bf16[8192,896]{1,0:T(8,128)(2,1)} %gate_weight.1, bf16[8192,896]{1,0:T(8,128)(2,1)} %up_weight.1, bf16[1,64,8192]{2,1,0:T(8,128)(2,1)} %adapter_in.1, ...), custom_call_target="tpu_custom_call" | custom-call | tf_op jit(solution)/shard_map/gated_input/pallas_call | solution.py:326
  56.7 2.0 %copy.10 = bf16[384,896]{1,0:T(8,128)(2,1)} copy(bf16[384,896]{1,0:T(8,128)(2,1)} %gated_input.1) | data formatting | bytes 1376256

commit v4 on v3

--- a/solution.py
+++ b/solution.py
@@ -111,12 +111,10 @@
         sign = 1 - 2 * way
         return (pos - sign * step + 2 * chips) % chips
 
-    def send_own(win):
+    def send_own(way):
         for cut in range(PARTS):
-            for way in range(2):
-                ring_copy(way, win, cut, 0).start()
-        for way in range(2):
-            pair_copy(core, way, win, 0).start()
+            ring_copy(way, 0, cut, 0).start()
+        pair_copy(core, way, 0, 0).start()
 
     for win in range(WINDOWS):
         for way in range(2):
@@ -129,8 +127,7 @@
             gathered[core, way, win, :chip_rows, :] = jnp.concatenate(
                 [first, second], axis=0
             ).astype(jnp.bfloat16)
-        if win == 0:
-            send_own(0)
+            send_own(way)
 
     acc[...] = jnp.zeros_like(acc)
     low_acc[...] = jnp.zeros_like(low_acc)

time: 58.9 us -> 58.9 us (level)
  no operation moved by 1% of the time
where the time goes in v4:
time: 58.9 us; the launch traced here: 58.7 us
  Pallas kernels  56.7 us (96%)
  local copies, waits for them, and re-layouts  2 us (3%)
    pallas_call x1, Pallas kernels, fused(): pl.pallas_call(functools.partial(kernel, n, seg_adapter.shape[0]), out_sh...  56.7 us
    unnamed x1, local copies, waits for them, and re-layouts  2 us

profile of v4, /device:TPU:0, one launch (start us, length us, event | category | flops | bytes accessed | tf_op | source)
XLA Modules:
  0.0 58.7 jit_solution(17867777419039370023)
XLA Ops:
  0.0 56.7 %gated_input.1 = bf16[384,896]{1,0:T(8,128)(2,1)} custom-call(s32[3]{0:T(128)} %seg_adapter.1, s32[16]{0:T(128)} %holder_slot.1, s32[3]{0:T(128)} %seg_length.1, bf16[24,8192]{1,0:T(8,128)(2,1)} %tokens.1, bf16[8192,896]{1,0:T(8,128)(2,1)} %gate_weight.1, bf16[8192,896]{1,0:T(8,128)(2,1)} %up_weight.1, bf16[1,64,8192]{2,1,0:T(8,128)(2,1)} %adapter_in.1, ...), custom_call_target="tpu_custom_call" | custom-call | tf_op jit(solution)/shard_map/gated_input/pallas_call | solution.py:323
  56.7 2.0 %copy.10 = bf16[384,896]{1,0:T(8,128)(2,1)} copy(bf16[384,896]{1,0:T(8,128)(2,1)} %gated_input.1) | data formatting | bytes 1376256
